TPU v7x, 32 devices: a whole 2x2x4 slice. The times are simulated.
32 devices in a mesh: dp: 4 (over z), context: 4 (over y, x), tensor: 2 (over core).
Axes of the slice: x: 2, y: 2, z: 4, core: 2. Of those that a mesh axis runs over, the one named last changes fastest.
Arguments:
- queries: bfloat16 [2048, 4096], P(('dp', 'context'), 'tensor'), parts along dimension 0, may hold values from -6 to 6
- keys: bfloat16 [2048, 1024], P(('dp', 'context'), 'tensor'), parts along dimension 0, may hold values from -6 to 6
- values: bfloat16 [2048, 1024], P(('dp', 'context'), 'tensor'), parts along dimension 0, may hold values from -6 to 6
- order: int32 [2048], P('dp'), parts along dimension 0, may hold values from 0 to 511, as said below
- out_weight: bfloat16 [4096, 4096], P('tensor', 'context'), may hold values from -0.125 to 0.125
Outputs:
- output: bfloat16 [2048, 4096], P(('dp', 'context'), 'tensor'), parts along dimension 0
There are 4 independent parts, one for each index of `dp`. A program takes and returns all parts, laid end to end along the dimension named above; an argument that names none is the same for every part. Nothing has to cross between parts.
Inputs may be any that keep to these rules, and one draw needn't show every extreme that they name: A permutation of the positions; each aligned block of 128 rows holds 128 consecutive positions in increasing order, starting at a multiple of 128.
All inputs are finite; a program needn't handle non-finite values.
Results may differ from a plain program's by a relative error of at most 0.019.
Values may be sent and summed in bfloat16 or wider, within the bound.
A program may use at most 64 MiB of HBM per device.

v0:
```python
import math

import jax
import jax.numpy as jnp
from jax import lax
from jax.sharding import PartitionSpec as P

QUERY_HEADS = 32
KEY_VALUE_HEADS = 8
HEAD_SIZE = 128


def per_device(queries, keys, values, order, out_weight):
    row_count = queries.shape[0]
    local_groups = keys.shape[1] // HEAD_SIZE
    query_head_group = QUERY_HEADS // KEY_VALUE_HEADS
    score_scale = 1.0 / math.sqrt(HEAD_SIZE)
    first_row = lax.axis_index("context") * row_count
    query_pos = lax.dynamic_slice_in_dim(order, first_row, row_count, 0)
    stacked = queries.reshape(row_count, local_groups, query_head_group, HEAD_SIZE)
    stacked = stacked.transpose(1, 2, 0, 3).reshape(
        local_groups, query_head_group * row_count, HEAD_SIZE
    )
    stacked_pos = jnp.tile(query_pos, query_head_group)
    stacked_rows = query_head_group * row_count
    key_part = lax.all_gather(keys, "context", axis=0, tiled=True)
    value_part = lax.all_gather(values, "context", axis=0, tiled=True)
    key_count = key_part.shape[0]
    running_max = jnp.full((local_groups, stacked_rows), -1e30, jnp.float32)
    key_heads = key_part.reshape(key_count, local_groups, HEAD_SIZE)
    value_heads = value_part.reshape(key_count, local_groups, HEAD_SIZE)
    scores = (
        jnp.einsum("grd,kgd->grk", stacked, key_heads, preferred_element_type=jnp.float32)
        * score_scale
    )
    visible = order[None, None, :] <= stacked_pos[None, :, None]
    scores = jnp.where(visible, scores, -1e30)
    new_max = jnp.maximum(running_max, jnp.max(scores, axis=2))
    weights = jnp.where(visible, jnp.exp(scores - new_max[..., None]), 0.0)
    new_sum = jnp.sum(weights, axis=2)
    product = jnp.einsum(
        "grk,kgd->grd",
        weights.astype(jnp.bfloat16),
        value_heads,
        preferred_element_type=jnp.float32,
    )
    attended = (product / new_sum[..., None]).astype(jnp.bfloat16)
    attended = attended.reshape(local_groups, query_head_group, row_count, HEAD_SIZE).transpose(
        2, 0, 1, 3
    )
    attended = attended.reshape(row_count, local_groups * query_head_group * HEAD_SIZE)
    partial_out = jnp.dot(
        attended,
        lax.all_gather(out_weight, "context", axis=1, tiled=True),
        preferred_element_type=jnp.float32,
    )
    summed = lax.psum(partial_out.astype(jnp.bfloat16), "tensor").astype(jnp.float32)
    column_count = summed.shape[1] // lax.axis_size("tensor")
    mine = lax.dynamic_slice_in_dim(
        summed, lax.axis_index("tensor") * column_count, column_count, 1
    )
    return mine.astype(jnp.bfloat16)


def solution(mesh):
    placed = (
        P(("dp", "context"), "tensor"),
        P(("dp", "context"), "tensor"),
        P(("dp", "context"), "tensor"),
        P("dp"),
        P("tensor", "context"),
    )
    return jax.shard_map(
        per_device,
        mesh=mesh,
        in_specs=placed,
        out_specs=P(("dp", "context"), "tensor"),
        check_vma=False,
    )
```

profile of v0, /device:TPU:1, one launch (start us, length us, event | category | flops | bytes accessed | tf_op | source)
XLA Modules:
  0.0 208.5 jit_solution(18386593743090618850)
XLA Ops:
  6.5 0.0 copy-start
  6.5 0.0 copy-start.1
  6.5 0.0 copy-start.2
  6.5 0.0 copy-start.3
  6.5 0.0 all-gather.2.cloned.1.call-start
  6.6 0.7 all-gather.2.cloned.1.call-update
  7.3 0.0 all-reduce.2.cloned.1.call-start
  7.3 0.3 copy-done
  7.6 0.4 reshape.58
  7.9 0.1 copy.8
  8.1 0.0 copy-done.1
  8.1 0.1 copy.9
  8.2 0.0 copy-done.2
  8.2 0.1 copy.11
  8.4 0.0 copy-done.3
  8.4 0.1 dynamic_slice.6
  8.4 8.9 %all_gather.9 = bf16[512,512]{0,1:T(8,128)(2,1)S(1)} all-gather(bf16[128,512]{0,1:T(8,128)(2,1)S(1)} %copy.9), channel_id=1, replica_groups=mesh['dp'=4,'context'=4,'tensor'=2] {'context'}, dimensions={0}, use_global_device_ids=true | all-gather | bytes 655360 | tf_op jit(solution)/shard_map/all_gather | solution.py:26
  17.3 9.9 %all_gather.10 = bf16[512,512]{0,1:T(8,128)(2,1)S(1)} all-gather(bf16[128,512]{0,1:T(8,128)(2,1)S(1)} %copy.11), channel_id=1, replica_groups=mesh['dp'=4,'context'=4,'tensor'=2] {'context'}, dimensions={0}, use_global_device_ids=true | all-gather | bytes 655360 | tf_op jit(solution)/shard_map/all_gather | solution.py:27
  27.2 0.2 broadcast_compare_fusion
  27.4 1.0 fusion
  28.4 1.0 fusion.1
  29.5 1.8 divide_convert_fusion
  31.2 0.3 copy.14
  31.5 139.0 %all-gather.2.cloned.1.call-done = bf16[2048,4096]{1,0:T(8,128)(2,1)} async-done(((bf16[2048,1024]{1,0:T(8,128)(2,1)}), bf16[2048,4096]{1,0:T(8,128)(2,1)}) %all-gather.2.cloned.1.call-update) | async-done | bytes 16777232 | tf_op jit(solution)/shard_map/all_gather | solution.py:54
  170.5 9.1 %convolution_convert_fusion = bf16[128,4096]{1,0:T(8,128)(2,1)} fusion(bf16[128,2048]{0,1:T(8,128)(2,1)S(1)} %bitcast.15, bf16[2048,4096]{1,0:T(8,128)(2,1)} %all-gather.2.cloned.1.call-done), kind=kOutput, calls=%fused_computation | convolution fusion | flops 2148007936 | bytes 18350080 | tf_op jit(solution)/shard_map/dot_general | solution.py:52
  179.6 0.0 all-reduce.2.cloned.1.call-update
  179.6 20.2 %all-reduce.2.cloned.1.call-done = bf16[128,4096]{1,0:T(8,128)(2,1)} async-done(((bf16[128,4096]{1,0:T(8,128)(2,1)}), bf16[128,4096]{1,0:T(8,128)(2,1)}) %all-reduce.2.cloned.1.call-update) | async-done | bytes 1048592 | tf_op jit(solution)/shard_map/psum | solution.py:57
  199.8 1.9 convert_convert_fusion
  (2 shorter events, 0.0 us)
Async XLA Ops:
  6.5 1.0 copy-start
  6.5 1.6 copy-start.1
  6.5 1.7 copy-start.2
  6.5 1.8 copy-start.3
  6.5 164.0 %all-gather.2.cloned.1.call-start = ((), (), s32[]{:S(2)}) async-start(), calls=%async_computation | async-start | bytes 20971520 | tf_op jit(solution)/shard_map/all_gather | solution.py:54
  7.3 192.5 %all-reduce.2.cloned.1.call-start = ((), (), s32[]{:S(2)}) async-start(), calls=%async_computation.1 | async-start | bytes 2097152 | tf_op jit(solution)/shard_map/psum | solution.py:57
Sparse Core Ops, SparseCore 0:
  9.2 161.2 all-gather.1
  179.8 19.9 all-reduce.1
where the time goes:
time: 209 us
  waiting for transfers between devices  160 us (77%)
  blocking collectives  18.7 us (9%)
  between operations  13.5 us (6%)
  matrix products  11.9 us (6%)
  other arithmetic  3.14 us (2%)
    all_gather x1, waiting for transfers between devices, per_device(): lax.all_gather(out_weight, 'context', axis=1, tiled=True)  139 us
    psum x1, waiting for transfers between devices, per_device(): lax.psum(partial_out.astype(jnp.bfloat16), 'tensor').astype(jnp.float32)  20.2 us
    all_gather x1, blocking collectives, per_device(): value_part = lax.all_gather(values, 'context', axis=0, tiled=True)  9.9 us
    dot_general x1, matrix products, per_device(): jnp.dot(attended, lax.all_gather(out_weight, 'context', axis=1, tiled=Tru...  9.11 us
    all_gather x1, blocking collectives, per_device(): key_part = lax.all_gather(keys, 'context', axis=0, tiled=True)  8.85 us
  transfers between devices with their start and end apart: 2, of which 2 were waited for; matrix products, arithmetic and copies ran while one was open for 2% of the time, Pallas kernels for 0%

commit v1 on v0

v1 whole, which is shorter than its diff:
```python
import functools
import math

import jax
import jax.numpy as jnp
from jax import lax
from jax.experimental import pallas as pl
from jax.experimental.pallas import tpu as pltpu
from jax.sharding import PartitionSpec as P

QUERY_HEADS = 32
KEY_VALUE_HEADS = 8
HEAD_SIZE = 128
BLK = 128
GROUP = QUERY_HEADS // KEY_VALUE_HEADS
MASKED = -1e30


def plane(count):
    rows = 1 << ((count.bit_length() - 1) // 2)
    return rows, count // rows


def kernel(
    contexts,
    tensors,
    q_hbm,
    k_hbm,
    v_hbm,
    order_ref,
    w_hbm,
    out_ref,
    q_buf,
    k_buf,
    v_buf,
    w_buf,
    bias,
    att,
    acc,
    part,
    got,
    done,
    local_sem,
    send_sem,
    recv_sem,
    out_send_sem,
    out_recv_sem,
):
    high, wide = plane(contexts)
    rows = q_hbm.shape[0]
    groups = k_hbm.shape[1] // HEAD_SIZE
    span = GROUP * HEAD_SIZE
    half = span // 2
    share = rows // tensors
    columns = w_hbm.shape[1]
    ratio = contexts // tensors
    c = lax.axis_index("context")
    t = lax.axis_index("tensor")
    y, x = c // wide, lax.rem(c, wide)

    slots = [(0, 0)]
    slots += [(0, dx) for dx in range(1, wide)]
    slots += [(dy, 0) for dy in range(1, high)]
    direct = len(slots)
    slots += [(dy, dx) for dy in range(1, high) for dx in range(1, wide)]
    slot_of = {offset: i for i, offset in enumerate(slots)}
    row_peers = [(0, dx) for dx in range(1, wide)]
    column_peers = [(dy, 0) for dy in range(1, high)]

    def after(dy, dx):
        return lax.rem(y + dy, high) * wide + lax.rem(x + dx, wide)

    def before(dy, dx):
        return after(high - dy, wide - dx)

    sends = []

    def remote(src, dst, context, tensor):
        i = len(sends)
        copy = pltpu.make_async_remote_copy(
            src_ref=src,
            dst_ref=dst,
            send_sem=send_sem.at[i],
            recv_sem=recv_sem.at[i],
            device_id={"context": context, "tensor": tensor},
            device_id_type=pl.DeviceIdType.MESH,
        )
        copy.start()
        sends.append(copy)
        return copy

    locals_started = []

    def local(src, dst):
        copy = pltpu.make_async_copy(src, dst, local_sem.at[len(locals_started)])
        copy.start()
        locals_started.append(copy)
        return copy

    barrier = pltpu.get_barrier_semaphore()
    for dc in range(contexts):
        for dt in range(tensors):
            if dc or dt:
                pl.semaphore_signal(
                    barrier,
                    inc=1,
                    device_id={
                        "context": lax.rem(c + dc, contexts),
                        "tensor": lax.rem(t + dt, tensors),
                    },
                    device_id_type=pl.DeviceIdType.MESH,
                )

    def head_columns(g):
        return pl.ds(g * HEAD_SIZE, HEAD_SIZE)

    own_k = [local(k_hbm.at[:, head_columns(g)], k_buf.at[g, 0]) for g in range(groups)]
    own_v = [local(v_hbm.at[:, head_columns(g)], v_buf.at[g, 0]) for g in range(groups)]
    own_q = local(q_hbm, q_buf)
    own_w = [
        local(w_hbm.at[pl.ds(g * span, span)], w_buf.at[pl.ds(g * span, span)])
        for g in range(groups)
    ]

    pl.semaphore_wait(barrier, contexts * tensors - 1)

    k_in, v_in = {}, {}
    for g in range(groups):
        for offset in row_peers + column_peers:
            s = slot_of[offset]
            k_in[g, s] = remote(k_hbm.at[:, head_columns(g)], k_buf.at[g, s], after(*offset), t)
            v_in[g, s] = remote(v_hbm.at[:, head_columns(g)], v_buf.at[g, s], after(*offset), t)

    first = order_ref[c * BLK]
    i = lax.broadcasted_iota(jnp.int32, (rows, rows), 0)
    j = lax.broadcasted_iota(jnp.int32, (rows, rows), 1)
    bias[:, 0:rows] = jnp.where(j <= i, 0.0, MASKED).astype(jnp.float32)
    for s in range(1, contexts):
        theirs = order_ref[before(*slots[s]) * BLK]
        level = jnp.where(theirs < first, 0.0, MASKED).astype(jnp.float32)
        bias[:, s * rows : (s + 1) * rows] = jnp.full((rows, rows), level, jnp.float32)

    for g in range(groups):
        for offset in row_peers:
            s = slot_of[offset]
            k_in[g, s].wait_recv()
            for down in column_peers:
                d = slot_of[down[0], offset[1]]
                k_in[g, d] = remote(k_buf.at[g, s], k_buf.at[g, d], after(*down), t)
        for offset in column_peers:
            s = slot_of[offset]
            v_in[g, s].wait_recv()
            for across in row_peers:
                d = slot_of[offset[0], across[1]]
                v_in[g, d] = remote(v_buf.at[g, s], v_buf.at[g, d], after(*across), t)

    def attend(g):
        own_k[g].wait()
        own_v[g].wait()
        for s in range(1, contexts):
            if not (s < direct and slots[s][0] == 0):
                k_in[g, s].wait_recv()
            if not (s < direct and slots[s][1] == 0):
                v_in[g, s].wait_recv()
        k = k_buf[g].reshape(contexts * rows, HEAD_SIZE)
        v = v_buf[g].reshape(contexts * rows, HEAD_SIZE)
        for h in range(GROUP):
            at = g * span + h * HEAD_SIZE
            q = q_buf[:, at : at + HEAD_SIZE]
            scores = lax.dot_general(
                q, k, (((1,), (1,)), ((), ())), preferred_element_type=jnp.float32
            )
            scores = scores + bias[...]
            top = jnp.max(scores, axis=1, keepdims=True)
            weights = jnp.exp2((scores - top) * (math.log2(math.e) / math.sqrt(HEAD_SIZE)))
            total = jnp.sum(weights, axis=1, keepdims=True)
            mixed = jnp.dot(weights.astype(jnp.bfloat16), v, preferred_element_type=jnp.float32)
            att[0, :, at : at + HEAD_SIZE] = (mixed / total).astype(jnp.bfloat16)

    a_in = {}

    def pass_on(g):
        left = pl.ds(g * span, half)
        right = pl.ds(g * span + half, half)
        for offset in row_peers:
            s = slot_of[offset]
            a_in[g, s].wait_recv()
            for down in column_peers:
                d = slot_of[down[0], offset[1]]
                a_in[g, d, 0] = remote(
                    att.at[s, :, left], att.at[d, :, left], after(*down), t
                )
        for offset in column_peers:
            s = slot_of[offset]
            a_in[g, s].wait_recv()
            for across in row_peers:
                d = slot_of[offset[0], across[1]]
                a_in[g, d, 1] = remote(
                    att.at[s, :, right], att.at[d, :, right], after(*across), t
                )

    def project(g, low, up):
        depth = slice(g * span, (g + 1) * span)
        lhs = att[low:up, :, depth].reshape((up - low) * rows, span)
        product = jnp.dot(lhs, w_buf[depth, :], preferred_element_type=jnp.float32)
        product = product.reshape(up - low, rows, columns)
        if g == 0:
            acc[low:up] = product
        else:
            acc[low:up] += product

    own_q.wait()
    for g in range(groups):
        attend(g)
        here = pl.ds(g * span, span)
        for offset in row_peers + column_peers:
            s = slot_of[offset]
            a_in[g, s] = remote(att.at[0, :, here], att.at[s, :, here], after(*offset), t)
        if g >= 2:
            pass_on(g - 2)
    for g in range(max(groups - 2, 0), groups):
        pass_on(g)
        if g == groups - 2 or groups == 1:
            for earlier in range(0, g):
                own_w[earlier].wait()
                project(earlier, 0, direct)
        own_w[g].wait()
        project(g, 0, direct)

    p_in = {}

    def exchange(s):
        part[s] = acc[s].astype(jnp.bfloat16)
        for dt in range(1, tensors):
            other = lax.rem(t + dt, tensors)
            theirs = pl.ds(pl.multiple_of(other * share, share), share)
            p_in[s, dt] = remote(part.at[s, theirs], got.at[s, dt - 1], c, other)

    mine = pl.ds(pl.multiple_of(t * share, share), share)
    target = c // ratio
    out_at = out_ref.at[mine, pl.ds(pl.multiple_of(lax.rem(c, ratio) * columns, columns), columns)]
    piece = lax.rem(c, ratio) * tensors + t
    out_sends = []

    def finish(s):
        total = acc[s, mine]
        for dt in range(1, tensors):
            p_in[s, dt].wait_recv()
            total = total + got[s, dt - 1].astype(jnp.float32)
        done[s] = total.astype(jnp.bfloat16)
        copy = pltpu.make_async_remote_copy(
            src_ref=done.at[s],
            dst_ref=out_at,
            send_sem=out_send_sem.at[s],
            recv_sem=out_recv_sem.at[piece],
            device_id={"context": before(*slots[s]), "tensor": target},
            device_id_type=pl.DeviceIdType.MESH,
        )
        if s:
            copy.start()
        else:

            @pl.when(target == t)
            def _():
                pltpu.make_async_copy(done.at[s], out_at, out_recv_sem.at[piece]).start()

            @pl.when(target != t)
            def _():
                copy.start()

        out_sends.append(copy)

    for s in range(1, direct):
        exchange(s)
    exchange(0)
    for g in range(groups - 1):
        for s in range(direct, contexts):
            a_in[g, s, 0].wait_recv()
            a_in[g, s, 1].wait_recv()
        project(g, direct, contexts)
        if g == 0:
            for s in range(1, direct):
                finish(s)
    if groups == 1:
        for s in range(1, direct):
            finish(s)
    g = groups - 1
    for s in range(direct, contexts):
        a_in[g, s, 0].wait_recv()
        a_in[g, s, 1].wait_recv()
    project(g, direct, contexts)
    for s in range(direct, contexts):
        exchange(s)
    for s in range(direct, contexts):
        finish(s)
    finish(0)

    for n in range(ratio):
        for m in range(tensors):
            landed = out_ref.at[pl.ds(m * share, share), pl.ds(n * columns, columns)]
            pltpu.make_async_copy(landed, landed, out_recv_sem.at[n * tensors + m]).wait()
    for copy in out_sends[:-1]:
        copy.wait_send()

    @pl.when(target != t)
    def _():
        out_sends[-1].wait_send()

    for copy in sends:
        copy.wait_send()


def per_device(contexts, tensors, queries, keys, values, order, out_weight):
    rows, width = queries.shape
    groups = keys.shape[1] // HEAD_SIZE
    columns = out_weight.shape[1]
    share = rows // tensors
    high, wide = plane(contexts)
    near = high + wide - 2
    far = (high - 1) * (wide - 1)
    copies = groups * (3 * near + 4 * far) + contexts * (tensors - 1)
    anywhere = pl.BlockSpec(memory_space=pl.ANY)
    bf16, f32 = jnp.bfloat16, jnp.float32
    return pl.pallas_call(
        functools.partial(kernel, contexts, tensors),
        out_shape=jax.ShapeDtypeStruct((rows, contexts // tensors * columns), bf16),
        in_specs=[
            anywhere,
            anywhere,
            anywhere,
            pl.BlockSpec(memory_space=pltpu.SMEM),
            anywhere,
        ],
        out_specs=anywhere,
        scratch_shapes=[
            pltpu.VMEM((rows, width), bf16),
            pltpu.VMEM((groups, contexts, rows, HEAD_SIZE), bf16),
            pltpu.VMEM((groups, contexts, rows, HEAD_SIZE), bf16),
            pltpu.VMEM(out_weight.shape, bf16),
            pltpu.VMEM((rows, contexts * rows), f32),
            pltpu.VMEM((contexts, rows, width), bf16),
            pltpu.VMEM((contexts, rows, columns), f32),
            pltpu.VMEM((contexts, rows, columns), bf16),
            pltpu.VMEM((contexts, tensors - 1, share, columns), bf16),
            pltpu.VMEM((contexts, share, columns), bf16),
            pltpu.SemaphoreType.DMA((3 * groups + 1,)),
            pltpu.SemaphoreType.DMA((copies,)),
            pltpu.SemaphoreType.DMA((copies,)),
            pltpu.SemaphoreType.DMA((contexts,)),
            pltpu.SemaphoreType.DMA((contexts,)),
        ],
        compiler_params=pltpu.CompilerParams(
            collective_id=0, has_side_effects=True, vmem_limit_bytes=48 * 1024 * 1024
        ),
        name="attend_and_project",
    )(queries, keys, values, order, out_weight)


def solution(mesh):
    placed = (
        P(("dp", "context"), "tensor"),
        P(("dp", "context"), "tensor"),
        P(("dp", "context"), "tensor"),
        P("dp"),
        P("tensor", "context"),
    )
    return jax.shard_map(
        functools.partial(per_device, mesh.shape["context"], mesh.shape["tensor"]),
        mesh=mesh,
        in_specs=placed,
        out_specs=P(("dp", "context"), "tensor"),
        check_vma=False,
    )
```

time: 209 us -> 46.6 us (0.22)
  waiting for transfers between devices: 160 us -> 0 us
  Pallas kernels: 0 us -> 39.8 us
  blocking collectives: 18.7 us -> 0 us
  between operations: 13.5 us -> 0.01 us
  matrix products: 11.9 us -> 0 us
  local copies, waits for them, and re-layouts: 1.36 us -> 6.51 us
  other arithmetic: 3.14 us -> 0 us
    all_gather x1 -> x0, waiting for transfers between devices: 139 us -> none  [per_device(): lax.all_gather(out_weight, 'context', axis=1, tiled=True)]
    pallas_call x0 -> x1, Pallas kernels: none -> 39.8 us  [per_device(): pl.pallas_call(functools.partial(kernel, contexts, tensors), out_shape=ja...]
    psum x1 -> x0, waiting for transfers between devices: 20.2 us -> none  [per_device(): lax.psum(partial_out.astype(jnp.bfloat16), 'tensor').astype(jnp.float32)]
    all_gather x2 -> x0, blocking collectives: 18.7 us -> none  [the longest x1 9.9 us: per_device(): value_part = lax.all_gather(values, 'context', axis=0, tiled=True)]
    dot_general x3 -> x0, matrix products: 11.9 us -> none  [the longest x1 9.11 us: per_device(): jnp.dot(attended, lax.all_gather(out_weight, 'context', axis=1, tiled=Tru...]
    unnamed x10 -> x11, local copies, waits for them, and re-layouts: 0.5 us -> 6.51 us
  transfers between devices with their start and end apart: 2 -> 0, of which waited for: 2 -> 0; matrix products, arithmetic and copies ran while one was open for 2% -> 0% of each run, Pallas kernels for 0% -> 0%
where the time goes in v1:
time: 46.6 us; the launch traced here: 46.3 us
  Pallas kernels  39.8 us (85%)
  local copies, waits for them, and re-layouts  6.51 us (14%)
    pallas_call x1, Pallas kernels, per_device(): pl.pallas_call(functools.partial(kernel, contexts, tensors), out_shape=ja...  39.8 us
    unnamed x11, local copies, waits for them, and re-layouts  6.51 us

profile of v1, /device:TPU:1, one launch (start us, length us, event | category | flops | bytes accessed | tf_op | source)
XLA Modules:
  0.0 46.3 jit_solution(17643040444319412848)
XLA Ops:
  0.0 0.0 copy-start
  0.0 2.2 %copy-done = bf16[2048,1024]{1,0:T(8,128)(2,1)S(1)} copy-done((bf16[2048,1024]{1,0:T(8,128)(2,1)S(1)}, bf16[2048,1024]{1,0:T(8,128)(2,1)}, u32[]{:S(2)}) %copy-start) | copy-done | bytes 4194328
  2.2 0.0 copy-start.1
  2.2 1.0 %copy-done.1 = bf16[128,2048]{1,0:T(8,128)(2,1)S(1)} copy-done((bf16[128,2048]{1,0:T(8,128)(2,1)S(1)}, bf16[128,2048]{1,0:T(8,128)(2,1)}, u32[]{:S(2)}) %copy-start.1) | copy-done | bytes 524312
  3.2 0.0 copy-start.2
  3.2 0.9 %copy-done.2 = bf16[128,512]{1,0:T(8,128)(2,1)S(1)} copy-done((bf16[128,512]{1,0:T(8,128)(2,1)S(1)}, bf16[128,512]{1,0:T(8,128)(2,1)}, u32[]{:S(2)}) %copy-start.2) | copy-done | bytes 131096
  4.1 0.0 copy-start.3
  4.1 0.9 %copy-done.3 = bf16[128,512]{1,0:T(8,128)(2,1)S(1)} copy-done((bf16[128,512]{1,0:T(8,128)(2,1)S(1)}, bf16[128,512]{1,0:T(8,128)(2,1)}, u32[]{:S(2)}) %copy-start.3) | copy-done | bytes 131096
  5.0 0.0 copy-start.4
  5.0 0.7 %copy-done.4 = s32[512]{0:T(512)S(1)} copy-done((s32[512]{0:T(512)S(1)}, s32[512]{0:T(512)}, u32[]{:S(2)}) %copy-start.4) | copy-done | bytes 2072
  5.7 39.8 %attend_and_project.1 = bf16[128,2048]{1,0:T(8,128)(2,1)S(1)} custom-call(bf16[128,2048]{1,0:T(8,128)(2,1)S(1)} %copy-done.1, bf16[128,512]{1,0:T(8,128)(2,1)S(1)} %copy-done.2, bf16[128,512]{1,0:T(8,128)(2,1)S(1)} %copy-done.3, s32[512]{0:T(512)S(1)} %copy-done.4, bf16[2048,1024]{1,0:T(8,128)(2,1)S(1)} %copy-done), custom_call_target="tpu_custom_call" | custom-call | tf_op jit(solution)/shard_map/attend_and_project/pallas_call | solution.py:324
  45.5 0.8 %copy.7 = bf16[128,2048]{1,0:T(8,128)(2,1)} copy(bf16[128,2048]{1,0:T(8,128)(2,1)S(1)} %attend_and_project.1) | data formatting | bytes 1048576
Async XLA Ops:
  0.0 2.2 %copy-start = (bf16[2048,1024]{1,0:T(8,128)(2,1)S(1)}, bf16[2048,1024]{1,0:T(8,128)(2,1)}, u32[]{:S(2)}) copy-start(bf16[2048,1024]{1,0:T(8,128)(2,1)} %w_hbm.1) | copy-start | bytes 12582916
  2.2 1.0 %copy-start.1 = (bf16[128,2048]{1,0:T(8,128)(2,1)S(1)}, bf16[128,2048]{1,0:T(8,128)(2,1)}, u32[]{:S(2)}) copy-start(bf16[128,2048]{1,0:T(8,128)(2,1)} %q_hbm.1) | copy-start | bytes 1572868
  3.2 0.9 %copy-start.2 = (bf16[128,512]{1,0:T(8,128)(2,1)S(1)}, bf16[128,512]{1,0:T(8,128)(2,1)}, u32[]{:S(2)}) copy-start(bf16[128,512]{1,0:T(8,128)(2,1)} %k_hbm.1) | copy-start | bytes 393220
  4.1 0.9 %copy-start.3 = (bf16[128,512]{1,0:T(8,128)(2,1)S(1)}, bf16[128,512]{1,0:T(8,128)(2,1)}, u32[]{:S(2)}) copy-start(bf16[128,512]{1,0:T(8,128)(2,1)} %v_hbm.1) | copy-start | bytes 393220
  5.0 0.7 %copy-start.4 = (s32[512]{0:T(512)S(1)}, s32[512]{0:T(512)}, u32[]{:S(2)}) copy-start(s32[512]{0:T(512)} %order_ref.1) | copy-start | bytes 6148

commit v2 on v1

--- a/solution.py
+++ b/solution.py
@@ -350,7 +350,7 @@
             pltpu.SemaphoreType.DMA((contexts,)),
         ],
         compiler_params=pltpu.CompilerParams(
-            collective_id=0, has_side_effects=True, vmem_limit_bytes=48 * 1024 * 1024
+            collective_id=0, has_side_effects=True, vmem_limit_bytes=64 * 1024 * 1024
         ),
         name="attend_and_project",
     )(queries, keys, values, order, out_weight)

time: 46.6 us -> 42.3 us (0.908)
  local copies, waits for them, and re-layouts: 6.51 us -> 1.88 us
    unnamed x11 -> x1, local copies, waits for them, and re-layouts: 6.51 us -> 1.88 us
    pallas_call x1, Pallas kernels: 39.8 us -> 40.2 us  [per_device(): pl.pallas_call(functools.partial(kernel, contexts, tensors), out_shape=ja...]
where the time goes in v2:
time: 42.3 us; the launch traced here: 42.1 us
  Pallas kernels  40.2 us (95%)
  local copies, waits for them, and re-layouts  1.88 us (4%)
    pallas_call x1, Pallas kernels, per_device(): pl.pallas_call(functools.partial(kernel, contexts, tensors), out_shape=ja...  40.2 us
    unnamed x1, local copies, waits for them, and re-layouts  1.88 us

profile of v2, /device:TPU:1, one launch (start us, length us, event | category | flops | bytes accessed | tf_op | source)
XLA Modules:
  0.0 42.1 jit_solution(12455501949153499600)
XLA Ops:
  0.0 40.2 %attend_and_project.1 = bf16[128,2048]{1,0:T(8,128)(2,1)} custom-call(bf16[128,2048]{1,0:T(8,128)(2,1)} %q_hbm.1, bf16[128,512]{1,0:T(8,128)(2,1)} %k_hbm.1, bf16[128,512]{1,0:T(8,128)(2,1)} %v_hbm.1, s32[512]{0:T(512)} %order_ref.1, bf16[2048,1024]{1,0:T(8,128)(2,1)} %w_hbm.1), custom_call_target="tpu_custom_call" | custom-call | tf_op jit(solution)/shard_map/attend_and_project/pallas_call | solution.py:324
  40.3 1.9 %copy.7 = bf16[128,2048]{1,0:T(8,128)(2,1)} copy(bf16[128,2048]{1,0:T(8,128)(2,1)} %attend_and_project.1) | data formatting | bytes 1048576

commit v3 on v2

--- a/solution.py
+++ b/solution.py
@@ -31,8 +31,7 @@
     w_hbm,
     out_ref,
     q_buf,
-    k_buf,
-    v_buf,
+    kv_buf,
     w_buf,
     bias,
     att,
@@ -114,8 +113,10 @@
     def head_columns(g):
         return pl.ds(g * HEAD_SIZE, HEAD_SIZE)
 
-    own_k = [local(k_hbm.at[:, head_columns(g)], k_buf.at[g, 0]) for g in range(groups)]
-    own_v = [local(v_hbm.at[:, head_columns(g)], v_buf.at[g, 0]) for g in range(groups)]
+    own_kv = []
+    for g in range(groups):
+        own_k = local(k_hbm.at[:, head_columns(g)], kv_buf.at[g, 0, 0])
+        own_kv.append((own_k, local(v_hbm.at[:, head_columns(g)], kv_buf.at[g, 0, 1])))
     own_q = local(q_hbm, q_buf)
     own_w = [
         local(w_hbm.at[pl.ds(g * span, span)], w_buf.at[pl.ds(g * span, span)])
@@ -124,12 +125,31 @@
 
     pl.semaphore_wait(barrier, contexts * tensors - 1)
 
-    k_in, v_in = {}, {}
-    for g in range(groups):
+    kv_in, k_far, v_far = {}, {}, {}
+
+    def send_group(g):
+        for copy in own_kv[g]:
+            copy.wait()
         for offset in row_peers + column_peers:
             s = slot_of[offset]
-            k_in[g, s] = remote(k_hbm.at[:, head_columns(g)], k_buf.at[g, s], after(*offset), t)
-            v_in[g, s] = remote(v_hbm.at[:, head_columns(g)], v_buf.at[g, s], after(*offset), t)
+            kv_in[g, s] = remote(kv_buf.at[g, 0], kv_buf.at[g, s], after(*offset), t)
+
+    def pass_group(g):
+        for offset in row_peers:
+            s = slot_of[offset]
+            kv_in[g, s].wait_recv()
+            for down in column_peers:
+                d = slot_of[down[0], offset[1]]
+                k_far[g, d] = remote(kv_buf.at[g, s, 0], kv_buf.at[g, d, 0], after(*down), t)
+        for offset in column_peers:
+            s = slot_of[offset]
+            kv_in[g, s].wait_recv()
+            for across in row_peers:
+                d = slot_of[offset[0], across[1]]
+                v_far[g, d] = remote(kv_buf.at[g, s, 1], kv_buf.at[g, d, 1], after(*across), t)
+
+    for g in range(min(2, groups)):
+        send_group(g)
 
     first = order_ref[c * BLK]
     i = lax.broadcasted_iota(jnp.int32, (rows, rows), 0)
@@ -140,30 +160,12 @@
         level = jnp.where(theirs < first, 0.0, MASKED).astype(jnp.float32)
         bias[:, s * rows : (s + 1) * rows] = jnp.full((rows, rows), level, jnp.float32)
 
-    for g in range(groups):
-        for offset in row_peers:
-            s = slot_of[offset]
-            k_in[g, s].wait_recv()
-            for down in column_peers:
-                d = slot_of[down[0], offset[1]]
-                k_in[g, d] = remote(k_buf.at[g, s], k_buf.at[g, d], after(*down), t)
-        for offset in column_peers:
-            s = slot_of[offset]
-            v_in[g, s].wait_recv()
-            for across in row_peers:
-                d = slot_of[offset[0], across[1]]
-                v_in[g, d] = remote(v_buf.at[g, s], v_buf.at[g, d], after(*across), t)
-
     def attend(g):
-        own_k[g].wait()
-        own_v[g].wait()
-        for s in range(1, contexts):
-            if not (s < direct and slots[s][0] == 0):
-                k_in[g, s].wait_recv()
-            if not (s < direct and slots[s][1] == 0):
-                v_in[g, s].wait_recv()
-        k = k_buf[g].reshape(contexts * rows, HEAD_SIZE)
-        v = v_buf[g].reshape(contexts * rows, HEAD_SIZE)
+        for s in range(direct, contexts):
+            k_far[g, s].wait_recv()
+            v_far[g, s].wait_recv()
+        k = kv_buf[g, :, 0].reshape(contexts * rows, HEAD_SIZE)
+        v = kv_buf[g, :, 1].reshape(contexts * rows, HEAD_SIZE)
         for h in range(GROUP):
             at = g * span + h * HEAD_SIZE
             q = q_buf[:, at : at + HEAD_SIZE]
@@ -175,52 +177,60 @@
             weights = jnp.exp2((scores - top) * (math.log2(math.e) / math.sqrt(HEAD_SIZE)))
             total = jnp.sum(weights, axis=1, keepdims=True)
             mixed = jnp.dot(weights.astype(jnp.bfloat16), v, preferred_element_type=jnp.float32)
-            att[0, :, at : at + HEAD_SIZE] = (mixed / total).astype(jnp.bfloat16)
+            side, place = divmod(h * HEAD_SIZE, half)
+            att[g, 0, side, :, place : place + HEAD_SIZE] = (mixed / total).astype(jnp.bfloat16)
 
     a_in = {}
 
-    def pass_on(g):
-        left = pl.ds(g * span, half)
-        right = pl.ds(g * span + half, half)
+    def send_attended(g):
+        for offset in row_peers + column_peers:
+            s = slot_of[offset]
+            a_in[g, s] = remote(att.at[g, 0], att.at[g, s], after(*offset), t)
+
+    def pass_attended(g):
         for offset in row_peers:
             s = slot_of[offset]
             a_in[g, s].wait_recv()
             for down in column_peers:
                 d = slot_of[down[0], offset[1]]
-                a_in[g, d, 0] = remote(
-                    att.at[s, :, left], att.at[d, :, left], after(*down), t
-                )
+                a_in[g, d, 0] = remote(att.at[g, s, 0], att.at[g, d, 0], after(*down), t)
         for offset in column_peers:
             s = slot_of[offset]
             a_in[g, s].wait_recv()
             for across in row_peers:
                 d = slot_of[offset[0], across[1]]
-                a_in[g, d, 1] = remote(
-                    att.at[s, :, right], att.at[d, :, right], after(*across), t
-                )
+                a_in[g, d, 1] = remote(att.at[g, s, 1], att.at[g, d, 1], after(*across), t)
 
     def project(g, low, up):
-        depth = slice(g * span, (g + 1) * span)
-        lhs = att[low:up, :, depth].reshape((up - low) * rows, span)
-        product = jnp.dot(lhs, w_buf[depth, :], preferred_element_type=jnp.float32)
+        product = 0.0
+        for side in range(2):
+            first_row = g * span + side * half
+            lhs = att[g, low:up, side].reshape((up - low) * rows, half)
+            product = product + jnp.dot(
+                lhs, w_buf[first_row : first_row + half, :], preferred_element_type=jnp.float32
+            )
         product = product.reshape(up - low, rows, columns)
         if g == 0:
             acc[low:up] = product
         else:
             acc[low:up] += product
 
-    own_q.wait()
     for g in range(groups):
-        attend(g)
-        here = pl.ds(g * span, span)
-        for offset in row_peers + column_peers:
-            s = slot_of[offset]
-            a_in[g, s] = remote(att.at[0, :, here], att.at[s, :, here], after(*offset), t)
-        if g >= 2:
-            pass_on(g - 2)
-    for g in range(max(groups - 2, 0), groups):
-        pass_on(g)
-        if g == groups - 2 or groups == 1:
+        pass_group(g)
+        if g + 2 < groups:
+            send_group(g + 2)
+        if g == 0:
+            own_q.wait()
+        if g >= 1:
+            attend(g - 1)
+            send_attended(g - 1)
+        if g >= 3:
+            pass_attended(g - 3)
+    attend(groups - 1)
+    send_attended(groups - 1)
+    for g in range(max(groups - 3, 0), groups):
+        pass_attended(g)
+        if g == max(groups - 3, 0):
             for earlier in range(0, g):
                 own_w[earlier].wait()
                 project(earlier, 0, direct)
@@ -318,7 +328,7 @@
     high, wide = plane(contexts)
     near = high + wide - 2
     far = (high - 1) * (wide - 1)
-    copies = groups * (3 * near + 4 * far) + contexts * (tensors - 1)
+    copies = groups * (2 * near + 4 * far) + contexts * (tensors - 1)
     anywhere = pl.BlockSpec(memory_space=pl.ANY)
     bf16, f32 = jnp.bfloat16, jnp.float32
     return pl.pallas_call(
@@ -334,11 +344,10 @@
         out_specs=anywhere,
         scratch_shapes=[
             pltpu.VMEM((rows, width), bf16),
-            pltpu.VMEM((groups, contexts, rows, HEAD_SIZE), bf16),
-            pltpu.VMEM((groups, contexts, rows, HEAD_SIZE), bf16),
+            pltpu.VMEM((groups, contexts, 2, rows, HEAD_SIZE), bf16),
             pltpu.VMEM(out_weight.shape, bf16),
             pltpu.VMEM((rows, contexts * rows), f32),
-            pltpu.VMEM((contexts, rows, width), bf16),
+            pltpu.VMEM((groups, contexts, 2, rows, width // groups // 2), bf16),
             pltpu.VMEM((contexts, rows, columns), f32),
             pltpu.VMEM((contexts, rows, columns), bf16),
             pltpu.VMEM((contexts, tensors - 1, share, columns), bf16),

time: 42.3 us -> 41.8 us (0.988)
  Pallas kernels: 40.2 us -> 39.7 us
    pallas_call x1, Pallas kernels: 40.2 us -> 39.7 us  [per_device(): pl.pallas_call(functools.partial(kernel, contexts, tensors), out_shape=ja...]
where the time goes in v3:
time: 41.8 us; the launch traced here: 41.6 us
  Pallas kernels  39.7 us (95%)
  local copies, waits for them, and re-layouts  1.88 us (4%)
    pallas_call x1, Pallas kernels, per_device(): pl.pallas_call(functools.partial(kernel, contexts, tensors), out_shape=ja...  39.7 us
    unnamed x1, local copies, waits for them, and re-layouts  1.88 us

profile of v3, /device:TPU:1, one launch (start us, length us, event | category | flops | bytes accessed | tf_op | source)
XLA Modules:
  0.0 41.6 jit_solution(9367438794700866563)
XLA Ops:
  0.0 39.7 %attend_and_project.1 = bf16[128,2048]{1,0:T(8,128)(2,1)} custom-call(bf16[128,2048]{1,0:T(8,128)(2,1)} %q_hbm.1, bf16[128,512]{1,0:T(8,128)(2,1)} %k_hbm.1, bf16[128,512]{1,0:T(8,128)(2,1)} %v_hbm.1, s32[512]{0:T(512)} %order_ref.1, bf16[2048,1024]{1,0:T(8,128)(2,1)} %w_hbm.1), custom_call_target="tpu_custom_call" | custom-call | tf_op jit(solution)/shard_map/attend_and_project/pallas_call | solution.py:334
  39.7 1.9 %copy.7 = bf16[128,2048]{1,0:T(8,128)(2,1)} copy(bf16[128,2048]{1,0:T(8,128)(2,1)} %attend_and_project.1) | data formatting | bytes 1048576

commit v4 on v3

--- a/solution.py
+++ b/solution.py
@@ -123,34 +123,6 @@
         for g in range(groups)
     ]
 
-    pl.semaphore_wait(barrier, contexts * tensors - 1)
-
-    kv_in, k_far, v_far = {}, {}, {}
-
-    def send_group(g):
-        for copy in own_kv[g]:
-            copy.wait()
-        for offset in row_peers + column_peers:
-            s = slot_of[offset]
-            kv_in[g, s] = remote(kv_buf.at[g, 0], kv_buf.at[g, s], after(*offset), t)
-
-    def pass_group(g):
-        for offset in row_peers:
-            s = slot_of[offset]
-            kv_in[g, s].wait_recv()
-            for down in column_peers:
-                d = slot_of[down[0], offset[1]]
-                k_far[g, d] = remote(kv_buf.at[g, s, 0], kv_buf.at[g, d, 0], after(*down), t)
-        for offset in column_peers:
-            s = slot_of[offset]
-            kv_in[g, s].wait_recv()
-            for across in row_peers:
-                d = slot_of[offset[0], across[1]]
-                v_far[g, d] = remote(kv_buf.at[g, s, 1], kv_buf.at[g, d, 1], after(*across), t)
-
-    for g in range(min(2, groups)):
-        send_group(g)
-
     first = order_ref[c * BLK]
     i = lax.broadcasted_iota(jnp.int32, (rows, rows), 0)
     j = lax.broadcasted_iota(jnp.int32, (rows, rows), 1)
@@ -159,6 +131,34 @@
         theirs = order_ref[before(*slots[s]) * BLK]
         level = jnp.where(theirs < first, 0.0, MASKED).astype(jnp.float32)
         bias[:, s * rows : (s + 1) * rows] = jnp.full((rows, rows), level, jnp.float32)
+
+    pl.semaphore_wait(barrier, contexts * tensors - 1)
+
+    kv_in, k_far, v_far = {}, {}, {}
+
+    def send_group(g):
+        for copy in own_kv[g]:
+            copy.wait()
+        for offset in row_peers + column_peers:
+            s = slot_of[offset]
+            kv_in[g, s] = remote(kv_buf.at[g, 0], kv_buf.at[g, s], after(*offset), t)
+
+    def pass_group(g):
+        for offset in row_peers:
+            s = slot_of[offset]
+            kv_in[g, s].wait_recv()
+            for down in column_peers:
+                d = slot_of[down[0], offset[1]]
+                k_far[g, d] = remote(kv_buf.at[g, s, 0], kv_buf.at[g, d, 0], after(*down), t)
+        for offset in column_peers:
+            s = slot_of[offset]
+            kv_in[g, s].wait_recv()
+            for across in row_peers:
+                d = slot_of[offset[0], across[1]]
+                v_far[g, d] = remote(kv_buf.at[g, s, 1], kv_buf.at[g, d, 1], after(*across), t)
+
+    for g in range(min(2, groups)):
+        send_group(g)
 
     def attend(g):
         for s in range(direct, contexts):
@@ -201,19 +201,18 @@
                 d = slot_of[offset[0], across[1]]
                 a_in[g, d, 1] = remote(att.at[g, s, 1], att.at[g, d, 1], after(*across), t)
 
-    def project(g, low, up):
+    def project(g, low, up, first=0, last=columns):
         product = 0.0
         for side in range(2):
             first_row = g * span + side * half
             lhs = att[g, low:up, side].reshape((up - low) * rows, half)
-            product = product + jnp.dot(
-                lhs, w_buf[first_row : first_row + half, :], preferred_element_type=jnp.float32
-            )
-        product = product.reshape(up - low, rows, columns)
+            rhs = w_buf[first_row : first_row + half, first:last]
+            product = product + jnp.dot(lhs, rhs, preferred_element_type=jnp.float32)
+        product = product.reshape(up - low, rows, last - first)
         if g == 0:
-            acc[low:up] = product
+            acc[low:up, :, first:last] = product
         else:
-            acc[low:up] += product
+            acc[low:up, :, first:last] += product
 
     for g in range(groups):
         pass_group(g)
@@ -238,83 +237,89 @@
         project(g, 0, direct)
 
     p_in = {}
-
-    def exchange(s):
-        part[s] = acc[s].astype(jnp.bfloat16)
+    strip = columns // 2
+
+    def exchange(s, n):
+        part[s, n] = acc[s, :, n * strip : (n + 1) * strip].astype(jnp.bfloat16)
         for dt in range(1, tensors):
             other = lax.rem(t + dt, tensors)
             theirs = pl.ds(pl.multiple_of(other * share, share), share)
-            p_in[s, dt] = remote(part.at[s, theirs], got.at[s, dt - 1], c, other)
+            p_in[s, n, dt] = remote(part.at[s, n, theirs], got.at[s, n, dt - 1], c, other)
 
     mine = pl.ds(pl.multiple_of(t * share, share), share)
     target = c // ratio
-    out_at = out_ref.at[mine, pl.ds(pl.multiple_of(lax.rem(c, ratio) * columns, columns), columns)]
-    piece = lax.rem(c, ratio) * tensors + t
-    out_sends = []
-
-    def finish(s):
-        total = acc[s, mine]
+    out_sends, own_sends = [], []
+
+    def finish(s, n):
+        total = acc[s, mine, n * strip : (n + 1) * strip]
         for dt in range(1, tensors):
-            p_in[s, dt].wait_recv()
-            total = total + got[s, dt - 1].astype(jnp.float32)
-        done[s] = total.astype(jnp.bfloat16)
+            p_in[s, n, dt].wait_recv()
+            total = total + got[s, n, dt - 1].astype(jnp.float32)
+        done[s, n] = total.astype(jnp.bfloat16)
+        left = pl.multiple_of(lax.rem(c, ratio) * columns + n * strip, strip)
+        out_at = out_ref.at[mine, pl.ds(left, strip)]
+        landed = out_recv_sem.at[(lax.rem(c, ratio) * tensors + t) * 2 + n]
         copy = pltpu.make_async_remote_copy(
-            src_ref=done.at[s],
+            src_ref=done.at[s, n],
             dst_ref=out_at,
-            send_sem=out_send_sem.at[s],
-            recv_sem=out_recv_sem.at[piece],
+            send_sem=out_send_sem.at[2 * s + n],
+            recv_sem=landed,
             device_id={"context": before(*slots[s]), "tensor": target},
             device_id_type=pl.DeviceIdType.MESH,
         )
         if s:
             copy.start()
+            out_sends.append(copy)
         else:
 
             @pl.when(target == t)
             def _():
-                pltpu.make_async_copy(done.at[s], out_at, out_recv_sem.at[piece]).start()
+                pltpu.make_async_copy(done.at[s, n], out_at, landed).start()
 
             @pl.when(target != t)
             def _():
                 copy.start()
 
-        out_sends.append(copy)
-
-    for s in range(1, direct):
-        exchange(s)
-    exchange(0)
-    for g in range(groups - 1):
+            own_sends.append(copy)
+
+    near = list(range(1, direct)) + [0]
+    for s in near:
+        for n in range(2):
+            exchange(s, n)
+    for g in range(groups):
+        last = g == groups - 1
+        if last:
+            for s in near:
+                for n in range(2):
+                    finish(s, n)
         for s in range(direct, contexts):
             a_in[g, s, 0].wait_recv()
             a_in[g, s, 1].wait_recv()
-        project(g, direct, contexts)
-        if g == 0:
-            for s in range(1, direct):
-                finish(s)
-    if groups == 1:
-        for s in range(1, direct):
-            finish(s)
-    g = groups - 1
-    for s in range(direct, contexts):
-        a_in[g, s, 0].wait_recv()
-        a_in[g, s, 1].wait_recv()
-    project(g, direct, contexts)
-    for s in range(direct, contexts):
-        exchange(s)
-    for s in range(direct, contexts):
-        finish(s)
-    finish(0)
-
-    for n in range(ratio):
-        for m in range(tensors):
-            landed = out_ref.at[pl.ds(m * share, share), pl.ds(n * columns, columns)]
-            pltpu.make_async_copy(landed, landed, out_recv_sem.at[n * tensors + m]).wait()
-    for copy in out_sends[:-1]:
+        if not last:
+            project(g, direct, contexts)
+        else:
+            for n in range(2):
+                project(g, direct, contexts, n * strip, (n + 1) * strip)
+                for s in range(direct, contexts):
+                    exchange(s, n)
+    for n in range(2):
+        for s in range(direct, contexts):
+            finish(s, n)
+
+    for i in range(contexts):
+        for n in range(2):
+            place, who = divmod(i, tensors)
+            landed = out_ref.at[
+                pl.ds(who * share, share), pl.ds(place * columns + n * strip, strip)
+            ]
+            pltpu.make_async_copy(landed, landed, out_recv_sem.at[2 * i + n]).wait()
+    for copy in out_sends:
         copy.wait_send()
 
     @pl.when(target != t)
     def _():
-        out_sends[-1].wait_send()
+        for copy in own_sends:
+            copy.wait_send()
 
     for copy in sends:
         copy.wait_send()
@@ -328,12 +333,12 @@
     high, wide = plane(contexts)
     near = high + wide - 2
     far = (high - 1) * (wide - 1)
-    copies = groups * (2 * near + 4 * far) + contexts * (tensors - 1)
+    copies = groups * (2 * near + 4 * far) + 2 * contexts * (tensors - 1)
     anywhere = pl.BlockSpec(memory_space=pl.ANY)
     bf16, f32 = jnp.bfloat16, jnp.float32
     return pl.pallas_call(
         functools.partial(kernel, contexts, tensors),
-        out_shape=jax.ShapeDtypeStruct((rows, contexts // tensors * columns), bf16),
+        out_shape=pltpu.VMEM((rows, contexts // tensors * columns), bf16),
         in_specs=[
             anywhere,
             anywhere,
@@ -349,17 +354,17 @@
             pltpu.VMEM((rows, contexts * rows), f32),
             pltpu.VMEM((groups, contexts, 2, rows, width // groups // 2), bf16),
             pltpu.VMEM((contexts, rows, columns), f32),
-            pltpu.VMEM((contexts, rows, columns), bf16),
-            pltpu.VMEM((contexts, tensors - 1, share, columns), bf16),
-            pltpu.VMEM((contexts, share, columns), bf16),
+            pltpu.VMEM((contexts, 2, rows, columns // 2), bf16),
+            pltpu.VMEM((contexts, 2, tensors - 1, share, columns // 2), bf16),
+            pltpu.VMEM((contexts, 2, share, columns // 2), bf16),
             pltpu.SemaphoreType.DMA((3 * groups + 1,)),
             pltpu.SemaphoreType.DMA((copies,)),
             pltpu.SemaphoreType.DMA((copies,)),
-            pltpu.SemaphoreType.DMA((contexts,)),
-            pltpu.SemaphoreType.DMA((contexts,)),
+            pltpu.SemaphoreType.DMA((2 * contexts,)),
+            pltpu.SemaphoreType.DMA((2 * contexts,)),
         ],
         compiler_params=pltpu.CompilerParams(
-            collective_id=0, has_side_effects=True, vmem_limit_bytes=64 * 1024 * 1024
+            collective_id=0, has_side_effects=True, vmem_limit_bytes=63 * 1024 * 1024
         ),
         name="attend_and_project",
     )(queries, keys, values, order, out_weight)

time: 41.8 us -> 40.9 us (0.978)
  local copies, waits for them, and re-layouts: 1.88 us -> 0.8 us
    unnamed x1, local copies, waits for them, and re-layouts: 1.88 us -> 0.8 us
where the time goes in v4:
time: 40.9 us; the launch traced here: 40.8 us
  Pallas kernels  40 us (98%)
  local copies, waits for them, and re-layouts  0.8 us (2%)
    pallas_call x1, Pallas kernels, per_device(): pl.pallas_call(functools.partial(kernel, contexts, tensors), out_shape=pl...  40 us

profile of v4, /device:TPU:1, one launch (start us, length us, event | category | flops | bytes accessed | tf_op | source)
XLA Modules:
  0.0 40.8 jit_solution(2224615356172172634)
XLA Ops:
  0.0 40.0 %attend_and_project.1 = bf16[128,2048]{1,0:T(8,128)(2,1)S(1)} custom-call(bf16[128,2048]{1,0:T(8,128)(2,1)} %q_hbm.1, bf16[128,512]{1,0:T(8,128)(2,1)} %k_hbm.1, bf16[128,512]{1,0:T(8,128)(2,1)} %v_hbm.1, s32[512]{0:T(512)} %order_ref.1, bf16[2048,1024]{1,0:T(8,128)(2,1)} %w_hbm.1), custom_call_target="tpu_custom_call" | custom-call | tf_op jit(solution)/shard_map/attend_and_project/pallas_call | solution.py:339
  40.0 0.8 %copy.7 = bf16[128,2048]{1,0:T(8,128)(2,1)} copy(bf16[128,2048]{1,0:T(8,128)(2,1)S(1)} %attend_and_project.1) | data formatting | bytes 1048576

commit v5 on v4

--- a/solution.py
+++ b/solution.py
@@ -166,40 +166,52 @@
             v_far[g, s].wait_recv()
         k = kv_buf[g, :, 0].reshape(contexts * rows, HEAD_SIZE)
         v = kv_buf[g, :, 1].reshape(contexts * rows, HEAD_SIZE)
-        for h in range(GROUP):
-            at = g * span + h * HEAD_SIZE
-            q = q_buf[:, at : at + HEAD_SIZE]
+        for side in range(2):
+            heads = [g * span + side * half + h * HEAD_SIZE for h in range(GROUP // 2)]
+            q = jnp.concatenate([q_buf[:, at : at + HEAD_SIZE] for at in heads], axis=0)
             scores = lax.dot_general(
                 q, k, (((1,), (1,)), ((), ())), preferred_element_type=jnp.float32
             )
-            scores = scores + bias[...]
+            scores = scores.reshape(GROUP // 2, rows, contexts * rows) + bias[...][None]
+            scores = scores.reshape(GROUP // 2 * rows, contexts * rows)
             top = jnp.max(scores, axis=1, keepdims=True)
             weights = jnp.exp2((scores - top) * (math.log2(math.e) / math.sqrt(HEAD_SIZE)))
             total = jnp.sum(weights, axis=1, keepdims=True)
             mixed = jnp.dot(weights.astype(jnp.bfloat16), v, preferred_element_type=jnp.float32)
-            side, place = divmod(h * HEAD_SIZE, half)
-            att[g, 0, side, :, place : place + HEAD_SIZE] = (mixed / total).astype(jnp.bfloat16)
+            mixed = (mixed / total).astype(jnp.bfloat16)
+            for h in range(GROUP // 2):
+                place = h * HEAD_SIZE
+                att[g, 0, side, :, place : place + HEAD_SIZE] = mixed[h * rows : (h + 1) * rows]
+            peers = row_peers + column_peers if side == 0 else column_peers + row_peers
+            for offset in peers:
+                s = slot_of[offset]
+                a_in[g, s, side] = remote(
+                    att.at[g, 0, side], att.at[g, s, side], after(*offset), t
+                )
 
     a_in = {}
-
-    def send_attended(g):
-        for offset in row_peers + column_peers:
-            s = slot_of[offset]
-            a_in[g, s] = remote(att.at[g, 0], att.at[g, s], after(*offset), t)
 
     def pass_attended(g):
         for offset in row_peers:
             s = slot_of[offset]
-            a_in[g, s].wait_recv()
+            a_in[g, s, 0].wait_recv()
             for down in column_peers:
                 d = slot_of[down[0], offset[1]]
                 a_in[g, d, 0] = remote(att.at[g, s, 0], att.at[g, d, 0], after(*down), t)
         for offset in column_peers:
             s = slot_of[offset]
-            a_in[g, s].wait_recv()
+            a_in[g, s, 1].wait_recv()
             for across in row_peers:
                 d = slot_of[offset[0], across[1]]
                 a_in[g, d, 1] = remote(att.at[g, s, 1], att.at[g, d, 1], after(*across), t)
+
+    def project_near(g):
+        own_w[g].wait()
+        for offset in row_peers:
+            a_in[g, slot_of[offset], 1].wait_recv()
+        for offset in column_peers:
+            a_in[g, slot_of[offset], 0].wait_recv()
+        project(g, 0, direct)
 
     def project(g, low, up, first=0, last=columns):
         product = 0.0
@@ -214,27 +226,24 @@
         else:
             acc[low:up, :, first:last] += product
 
-    for g in range(groups):
+    for g in range(min(2, groups)):
         pass_group(g)
         if g + 2 < groups:
             send_group(g + 2)
-        if g == 0:
-            own_q.wait()
-        if g >= 1:
-            attend(g - 1)
-            send_attended(g - 1)
-        if g >= 3:
-            pass_attended(g - 3)
-    attend(groups - 1)
-    send_attended(groups - 1)
-    for g in range(max(groups - 3, 0), groups):
+    own_q.wait()
+    attend(0)
+    for g in range(2, groups):
+        pass_group(g)
+    for g in range(1, groups):
+        attend(g)
+        if g >= 2:
+            pass_attended(g - 2)
+    for g in range(max(groups - 2, 0), groups):
         pass_attended(g)
-        if g == max(groups - 3, 0):
+        if g == max(groups - 2, 0):
             for earlier in range(0, g):
-                own_w[earlier].wait()
-                project(earlier, 0, direct)
-        own_w[g].wait()
-        project(g, 0, direct)
+                project_near(earlier)
+        project_near(g)
 
     p_in = {}
     strip = columns // 2
@@ -333,7 +342,7 @@
     high, wide = plane(contexts)
     near = high + wide - 2
     far = (high - 1) * (wide - 1)
-    copies = groups * (2 * near + 4 * far) + 2 * contexts * (tensors - 1)
+    copies = groups * (3 * near + 4 * far) + 2 * contexts * (tensors - 1)
     anywhere = pl.BlockSpec(memory_space=pl.ANY)
     bf16, f32 = jnp.bfloat16, jnp.float32
     return pl.pallas_call(

time: 40.9 us -> 40.7 us (level)
  no operation moved by 1% of the time
where the time goes in v5:
time: 40.7 us; the launch traced here: 40.6 us
  Pallas kernels  39.8 us (98%)
  local copies, waits for them, and re-layouts  0.8 us (2%)
    pallas_call x1, Pallas kernels, per_device(): pl.pallas_call(functools.partial(kernel, contexts, tensors), out_shape=pl...  39.8 us

profile of v5, /device:TPU:1, one launch (start us, length us, event | category | flops | bytes accessed | tf_op | source)
XLA Modules:
  0.0 40.6 jit_solution(18140267591992279019)
XLA Ops:
  0.0 39.8 %attend_and_project.1 = bf16[128,2048]{1,0:T(8,128)(2,1)S(1)} custom-call(bf16[128,2048]{1,0:T(8,128)(2,1)} %q_hbm.1, bf16[128,512]{1,0:T(8,128)(2,1)} %k_hbm.1, bf16[128,512]{1,0:T(8,128)(2,1)} %v_hbm.1, s32[512]{0:T(512)} %order_ref.1, bf16[2048,1024]{1,0:T(8,128)(2,1)} %w_hbm.1), custom_call_target="tpu_custom_call" | custom-call | tf_op jit(solution)/shard_map/attend_and_project/pallas_call | solution.py:348
  39.8 0.8 %copy.7 = bf16[128,2048]{1,0:T(8,128)(2,1)} copy(bf16[128,2048]{1,0:T(8,128)(2,1)S(1)} %attend_and_project.1) | data formatting | bytes 1048576

commit v6 on v5

--- a/solution.py
+++ b/solution.py
@@ -55,7 +55,10 @@
     ratio = contexts // tensors
     c = lax.axis_index("context")
     t = lax.axis_index("tensor")
+    square = high == wide and tensors % 2 == 0
+    flip = lax.rem(t, 2) if square else 0
     y, x = c // wide, lax.rem(c, wide)
+    y, x = y + flip * (x - y), x + flip * (y - x)
 
     slots = [(0, 0)]
     slots += [(0, dx) for dx in range(1, wide)]
@@ -67,7 +70,8 @@
     column_peers = [(dy, 0) for dy in range(1, high)]
 
     def after(dy, dx):
-        return lax.rem(y + dy, high) * wide + lax.rem(x + dx, wide)
+        u, v = lax.rem(y + dy, high), lax.rem(x + dx, wide)
+        return (1 - flip) * (u * wide + v) + flip * (v * wide + u)
 
     def before(dy, dx):
         return after(high - dy, wide - dx)
@@ -248,12 +252,16 @@
     p_in = {}
     strip = columns // 2
 
+    def twin(s, dt):
+        dy, dx = slots[s]
+        return slot_of[dx, dy] if square and dt % 2 else s
+
     def exchange(s, n):
         part[s, n] = acc[s, :, n * strip : (n + 1) * strip].astype(jnp.bfloat16)
         for dt in range(1, tensors):
             other = lax.rem(t + dt, tensors)
             theirs = pl.ds(pl.multiple_of(other * share, share), share)
-            p_in[s, n, dt] = remote(part.at[s, n, theirs], got.at[s, n, dt - 1], c, other)
+            p_in[s, n, dt] = remote(part.at[s, n, theirs], got.at[twin(s, dt), n, dt - 1], c, other)
 
     mine = pl.ds(pl.multiple_of(t * share, share), share)
     target = c // ratio
@@ -262,7 +270,7 @@
     def finish(s, n):
         total = acc[s, mine, n * strip : (n + 1) * strip]
         for dt in range(1, tensors):
-            p_in[s, n, dt].wait_recv()
+            p_in[twin(s, dt), n, dt].wait_recv()
             total = total + got[s, n, dt - 1].astype(jnp.float32)
         done[s, n] = total.astype(jnp.bfloat16)
         left = pl.multiple_of(lax.rem(c, ratio) * columns + n * strip, strip)

time: 40.7 us -> 40.9 us (level)
  no operation moved by 1% of the time
where the time goes in v6:
time: 40.9 us; the launch traced here: 40.8 us
  Pallas kernels  40 us (98%)
  local copies, waits for them, and re-layouts  0.8 us (2%)
    pallas_call x1, Pallas kernels, per_device(): pl.pallas_call(functools.partial(kernel, contexts, tensors), out_shape=pl...  40 us

profile of v6, /device:TPU:1, one launch (start us, length us, event | category | flops | bytes accessed | tf_op | source)
XLA Modules:
  0.0 40.8 jit_solution(4034839413333458511)
XLA Ops:
  0.0 40.0 %attend_and_project.1 = bf16[128,2048]{1,0:T(8,128)(2,1)S(1)} custom-call(bf16[128,2048]{1,0:T(8,128)(2,1)} %q_hbm.1, bf16[128,512]{1,0:T(8,128)(2,1)} %k_hbm.1, bf16[128,512]{1,0:T(8,128)(2,1)} %v_hbm.1, s32[512]{0:T(512)} %order_ref.1, bf16[2048,1024]{1,0:T(8,128)(2,1)} %w_hbm.1), custom_call_target="tpu_custom_call" | custom-call | tf_op jit(solution)/shard_map/attend_and_project/pallas_call | solution.py:356
  40.0 0.8 %copy.7 = bf16[128,2048]{1,0:T(8,128)(2,1)} copy(bf16[128,2048]{1,0:T(8,128)(2,1)S(1)} %attend_and_project.1) | data formatting | bytes 1048576

commit v7 on v5

--- a/solution.py
+++ b/solution.py
@@ -238,21 +238,14 @@
         attend(g)
         if g >= 2:
             pass_attended(g - 2)
-    for g in range(max(groups - 2, 0), groups):
-        pass_attended(g)
-        if g == max(groups - 2, 0):
-            for earlier in range(0, g):
-                project_near(earlier)
-        project_near(g)
-
     p_in = {}
     strip = columns // 2
 
     def exchange(s, n):
-        part[s, n] = acc[s, :, n * strip : (n + 1) * strip].astype(jnp.bfloat16)
         for dt in range(1, tensors):
             other = lax.rem(t + dt, tensors)
             theirs = pl.ds(pl.multiple_of(other * share, share), share)
+            part[s, n, theirs] = acc[s, theirs, n * strip : (n + 1) * strip].astype(jnp.bfloat16)
             p_in[s, n, dt] = remote(part.at[s, n, theirs], got.at[s, n, dt - 1], c, other)
 
     mine = pl.ds(pl.multiple_of(t * share, share), share)
@@ -291,26 +284,38 @@
 
             own_sends.append(copy)
 
-    near = list(range(1, direct)) + [0]
-    for s in near:
-        for n in range(2):
-            exchange(s, n)
-    for g in range(groups):
-        last = g == groups - 1
-        if last:
-            for s in near:
-                for n in range(2):
-                    finish(s, n)
+    def await_far(g):
         for s in range(direct, contexts):
             a_in[g, s, 0].wait_recv()
             a_in[g, s, 1].wait_recv()
-        if not last:
-            project(g, direct, contexts)
-        else:
-            for n in range(2):
-                project(g, direct, contexts, n * strip, (n + 1) * strip)
-                for s in range(direct, contexts):
-                    exchange(s, n)
+
+    def project_far(g):
+        await_far(g)
+        project(g, direct, contexts)
+
+    for g in range(groups - 2):
+        project_near(g)
+    for g in range(max(groups - 2, 0), groups):
+        pass_attended(g)
+        project_near(g)
+        if g < groups - 1:
+            for earlier in range(g):
+                project_far(earlier)
+    for s in list(range(1, direct)) + [0]:
+        for n in range(2):
+            exchange(s, n)
+    if groups > 1:
+        project_far(groups - 2)
+    for s in range(1, direct):
+        for n in range(2):
+            finish(s, n)
+    await_far(groups - 1)
+    for n in range(2):
+        project(groups - 1, direct, contexts, n * strip, (n + 1) * strip)
+        for s in range(direct, contexts):
+            exchange(s, n)
+    for n in range(2):
+        finish(0, n)
     for n in range(2):
         for s in range(direct, contexts):
             finish(s, n)

time: 40.7 us -> 41.9 us (1.029)
  Pallas kernels: 39.8 us -> 40.9 us
    pallas_call x1, Pallas kernels: 39.8 us -> 40.9 us  [per_device(): pl.pallas_call(functools.partial(kernel, contexts, tensors), out_shape=pl...]
where the time goes in v7:
time: 41.9 us; the launch traced here: 41.7 us
  Pallas kernels  40.9 us (98%)
  local copies, waits for them, and re-layouts  0.8 us (2%)
    pallas_call x1, Pallas kernels, per_device(): pl.pallas_call(functools.partial(kernel, contexts, tensors), out_shape=pl...  40.9 us

profile of v7, /device:TPU:1, one launch (start us, length us, event | category | flops | bytes accessed | tf_op | source)
XLA Modules:
  0.0 41.7 jit_solution(9322059956688213483)
XLA Ops:
  0.0 40.9 %attend_and_project.1 = bf16[128,2048]{1,0:T(8,128)(2,1)S(1)} custom-call(bf16[128,2048]{1,0:T(8,128)(2,1)} %q_hbm.1, bf16[128,512]{1,0:T(8,128)(2,1)} %k_hbm.1, bf16[128,512]{1,0:T(8,128)(2,1)} %v_hbm.1, s32[512]{0:T(512)} %order_ref.1, bf16[2048,1024]{1,0:T(8,128)(2,1)} %w_hbm.1), custom_call_target="tpu_custom_call" | custom-call | tf_op jit(solution)/shard_map/attend_and_project/pallas_call | solution.py:353
  40.9 0.8 %copy.7 = bf16[128,2048]{1,0:T(8,128)(2,1)} copy(bf16[128,2048]{1,0:T(8,128)(2,1)S(1)} %attend_and_project.1) | data formatting | bytes 1048576

commit v8 on v7

--- a/solution.py
+++ b/solution.py
@@ -293,29 +293,29 @@
         await_far(g)
         project(g, direct, contexts)
 
-    for g in range(groups - 2):
-        project_near(g)
     for g in range(max(groups - 2, 0), groups):
         pass_attended(g)
+        if g == groups - 2:
+            project_near(0)
+    for g in range(min(1, groups - 1), groups):
         project_near(g)
-        if g < groups - 1:
-            for earlier in range(g):
-                project_far(earlier)
     for s in list(range(1, direct)) + [0]:
         for n in range(2):
             exchange(s, n)
     if groups > 1:
-        project_far(groups - 2)
+        project_far(0)
     for s in range(1, direct):
         for n in range(2):
             finish(s, n)
+    for g in range(1, groups - 1):
+        project_far(g)
+    for n in range(2):
+        finish(0, n)
     await_far(groups - 1)
     for n in range(2):
         project(groups - 1, direct, contexts, n * strip, (n + 1) * strip)
         for s in range(direct, contexts):
             exchange(s, n)
-    for n in range(2):
-        finish(0, n)
     for n in range(2):
         for s in range(direct, contexts):
             finish(s, n)

time: 41.9 us -> 41.3 us (0.986)
  Pallas kernels: 40.9 us -> 40.4 us
    pallas_call x1, Pallas kernels: 40.9 us -> 40.4 us  [per_device(): pl.pallas_call(functools.partial(kernel, contexts, tensors), out_shape=pl...]
where the time goes in v8:
time: 41.3 us; the launch traced here: 41.2 us
  Pallas kernels  40.4 us (98%)
  local copies, waits for them, and re-layouts  0.8 us (2%)
    pallas_call x1, Pallas kernels, per_device(): pl.pallas_call(functools.partial(kernel, contexts, tensors), out_shape=pl...  40.4 us

profile of v8, /device:TPU:1, one launch (start us, length us, event | category | flops | bytes accessed | tf_op | source)
XLA Modules:
  0.0 41.2 jit_solution(11739925250522482609)
XLA Ops:
  0.0 40.4 %attend_and_project.1 = bf16[128,2048]{1,0:T(8,128)(2,1)S(1)} custom-call(bf16[128,2048]{1,0:T(8,128)(2,1)} %q_hbm.1, bf16[128,512]{1,0:T(8,128)(2,1)} %k_hbm.1, bf16[128,512]{1,0:T(8,128)(2,1)} %v_hbm.1, s32[512]{0:T(512)} %order_ref.1, bf16[2048,1024]{1,0:T(8,128)(2,1)} %w_hbm.1), custom_call_target="tpu_custom_call" | custom-call | tf_op jit(solution)/shard_map/attend_and_project/pallas_call | solution.py:353
  40.4 0.8 %copy.7 = bf16[128,2048]{1,0:T(8,128)(2,1)} copy(bf16[128,2048]{1,0:T(8,128)(2,1)S(1)} %attend_and_project.1) | data formatting | bytes 1048576

commit v9 on v8

--- a/solution.py
+++ b/solution.py
@@ -252,12 +252,14 @@
     target = c // ratio
     out_sends, own_sends = [], []
 
-    def finish(s, n):
+    def add_up(s, n):
         total = acc[s, mine, n * strip : (n + 1) * strip]
         for dt in range(1, tensors):
             p_in[s, n, dt].wait_recv()
             total = total + got[s, n, dt - 1].astype(jnp.float32)
         done[s, n] = total.astype(jnp.bfloat16)
+
+    def hand_over(s, n):
         left = pl.multiple_of(lax.rem(c, ratio) * columns + n * strip, strip)
         out_at = out_ref.at[mine, pl.ds(left, strip)]
         landed = out_recv_sem.at[(lax.rem(c, ratio) * tensors + t) * 2 + n]
@@ -302,23 +304,23 @@
     for s in list(range(1, direct)) + [0]:
         for n in range(2):
             exchange(s, n)
-    if groups > 1:
-        project_far(0)
-    for s in range(1, direct):
+    for g in range(groups - 1):
+        project_far(g)
+    for s in range(direct):
         for n in range(2):
-            finish(s, n)
-    for g in range(1, groups - 1):
-        project_far(g)
-    for n in range(2):
-        finish(0, n)
+            add_up(s, n)
     await_far(groups - 1)
+    for s in range(direct):
+        for n in range(2):
+            hand_over(s, n)
     for n in range(2):
         project(groups - 1, direct, contexts, n * strip, (n + 1) * strip)
         for s in range(direct, contexts):
             exchange(s, n)
     for n in range(2):
         for s in range(direct, contexts):
-            finish(s, n)
+            add_up(s, n)
+            hand_over(s, n)
 
     for i in range(contexts):
         for n in range(2):

time: 41.3 us -> 42.1 us (1.019)
  Pallas kernels: 40.4 us -> 41.2 us
    pallas_call x1, Pallas kernels: 40.4 us -> 41.2 us  [per_device(): pl.pallas_call(functools.partial(kernel, contexts, tensors), out_shape=pl...]
where the time goes in v9:
time: 42.1 us; the launch traced here: 42 us
  Pallas kernels  41.2 us (98%)
  local copies, waits for them, and re-layouts  0.8 us (2%)
    pallas_call x1, Pallas kernels, per_device(): pl.pallas_call(functools.partial(kernel, contexts, tensors), out_shape=pl...  41.2 us

profile of v9, /device:TPU:1, one launch (start us, length us, event | category | flops | bytes accessed | tf_op | source)
XLA Modules:
  0.0 42.0 jit_solution(6627949298045036885)
XLA Ops:
  0.0 41.2 %attend_and_project.1 = bf16[128,2048]{1,0:T(8,128)(2,1)S(1)} custom-call(bf16[128,2048]{1,0:T(8,128)(2,1)} %q_hbm.1, bf16[128,512]{1,0:T(8,128)(2,1)} %k_hbm.1, bf16[128,512]{1,0:T(8,128)(2,1)} %v_hbm.1, s32[512]{0:T(512)} %order_ref.1, bf16[2048,1024]{1,0:T(8,128)(2,1)} %w_hbm.1), custom_call_target="tpu_custom_call" | custom-call | tf_op jit(solution)/shard_map/attend_and_project/pallas_call | solution.py:355
  41.2 0.8 %copy.7 = bf16[128,2048]{1,0:T(8,128)(2,1)} copy(bf16[128,2048]{1,0:T(8,128)(2,1)S(1)} %attend_and_project.1) | data formatting | bytes 1048576

commit v10 on v5

--- a/solution.py
+++ b/solution.py
@@ -249,10 +249,10 @@
     strip = columns // 2
 
     def exchange(s, n):
-        part[s, n] = acc[s, :, n * strip : (n + 1) * strip].astype(jnp.bfloat16)
         for dt in range(1, tensors):
             other = lax.rem(t + dt, tensors)
             theirs = pl.ds(pl.multiple_of(other * share, share), share)
+            part[s, n, theirs] = acc[s, theirs, n * strip : (n + 1) * strip].astype(jnp.bfloat16)
             p_in[s, n, dt] = remote(part.at[s, n, theirs], got.at[s, n, dt - 1], c, other)
 
     mine = pl.ds(pl.multiple_of(t * share, share), share)
@@ -297,7 +297,7 @@
             exchange(s, n)
     for g in range(groups):
         last = g == groups - 1
-        if last:
+        if g == max(groups - 2, 0):
             for s in near:
                 for n in range(2):
                     finish(s, n)

time: 40.7 us -> 40.6 us (level)
  no operation moved by 1% of the time
where the time goes in v10:
time: 40.6 us; the launch traced here: 40.5 us
  Pallas kernels  39.7 us (98%)
  local copies, waits for them, and re-layouts  0.8 us (2%)
    pallas_call x1, Pallas kernels, per_device(): pl.pallas_call(functools.partial(kernel, contexts, tensors), out_shape=pl...  39.7 us

profile of v10, /device:TPU:1, one launch (start us, length us, event | category | flops | bytes accessed | tf_op | source)
XLA Modules:
  0.0 40.5 jit_solution(17976662285837719865)
XLA Ops:
  0.0 39.7 %attend_and_project.1 = bf16[128,2048]{1,0:T(8,128)(2,1)S(1)} custom-call(bf16[128,2048]{1,0:T(8,128)(2,1)} %q_hbm.1, bf16[128,512]{1,0:T(8,128)(2,1)} %k_hbm.1, bf16[128,512]{1,0:T(8,128)(2,1)} %v_hbm.1, s32[512]{0:T(512)} %order_ref.1, bf16[2048,1024]{1,0:T(8,128)(2,1)} %w_hbm.1), custom_call_target="tpu_custom_call" | custom-call | tf_op jit(solution)/shard_map/attend_and_project/pallas_call | solution.py:348
  39.7 0.8 %copy.7 = bf16[128,2048]{1,0:T(8,128)(2,1)} copy(bf16[128,2048]{1,0:T(8,128)(2,1)S(1)} %attend_and_project.1) | data formatting | bytes 1048576
